TPU v7x, 512 devices: a whole 4x8x8 slice. The times are simulated.
512 devices in a mesh: dp: 8 (over z), seq: 64 (over y, x, core).
Axes of the slice: x: 4, y: 8, z: 8, core: 2. Of those that a mesh axis runs over, the one named last changes fastest.
Arguments:
- tokens: bfloat16 [8, 8192, 1280], P('dp', 'seq'), may hold values from -6 to 6
- place: int32 [64, 128], P('seq'), may hold values from 0 to 127, each once within a row
- kernel: float32 [27, 1280], replicated, may hold values from -1.25 to 1.25
- proj_weight: bfloat16 [1280, 3840], P('seq'), may hold values from -0.15625 to 0.15625
- d_projected: bfloat16 [8, 8192, 3840], P('dp', 'seq'), may hold values from -6 to 6
Outputs:
- projected: bfloat16 [8, 8192, 3840], P('dp', 'seq')
- d_tokens: bfloat16 [8, 8192, 1280], P('dp', 'seq')
- d_kernel: float32 [27, 1280], replicated
Inputs may be any that keep to these rules, and one draw needn't show every extreme that they name: Each row of place holds every number 0 to 127 once.
All inputs are finite; a program needn't handle non-finite values.
Results may differ from a plain program's by a relative error of at most 0.005.
Values may be sent and summed in bfloat16 or wider, within the bound.
No kernel may reach another device: no remote copies, remote signals or barrier semaphores. Data moves between devices by JAX's collectives and lax.ppermute only.
A program may use at most 128 MiB of HBM per device.

v0:
```python
import jax
import jax.numpy as jnp
from jax import lax
from jax.sharding import PartitionSpec as P

INLINE = 8
CROSS = 8


def with_halo(value, sides, width):
    for axis, dim in sides:
        size, length = (lax.axis_size(axis), value.shape[dim])
        up = [(i, (i + 1) % size) for i in range(size - 1)]
        down = [(j, i) for i, j in up]
        last = lax.slice_in_dim(value, length - width, length, axis=dim)
        first = lax.slice_in_dim(value, 0, width, axis=dim)
        before = lax.ppermute(last, axis, up)
        after = lax.ppermute(first, axis, down)
        value = jnp.concatenate([before, value, after], axis=dim)
    return value


def brick_cells(landed, inverse):
    tokens_dev = inverse.shape[0]
    width = landed.shape[-1]
    slots = landed.reshape(tokens_dev, width)
    cells = jnp.take(slots, inverse, axis=0)
    return cells.reshape(tokens_dev // (INLINE * CROSS), INLINE, CROSS, width)


def scan_pieces(cells, order, count):
    width = cells.shape[-1]
    tokens_dev = order.shape[0]
    slots = jnp.take(cells.reshape(tokens_dev, width), order, axis=0)
    return slots.reshape(count, tokens_dev // count, width)


def to_bricks(rows, inverse, count):
    tokens_dev, width = rows.shape
    landed = lax.all_to_all(
        rows.reshape(count, tokens_dev // count, width),
        "seq",
        split_axis=0,
        concat_axis=0,
        tiled=True,
    )
    return brick_cells(landed, inverse)


def to_scan(cells, order, count):
    landed = lax.all_to_all(
        scan_pieces(cells, order, count), "seq", split_axis=0, concat_axis=0, tiled=True
    )
    return landed.reshape(order.shape[0], cells.shape[-1])


def with_faces(block):
    deeper = with_halo(block, (("seq", 0),), 1)
    return jnp.pad(deeper, ((0, 0), (1, 1), (1, 1), (0, 0)))


def window(field, depth_dev, start_z, start_i, start_c):
    return field[
        start_z : start_z + depth_dev, start_i : start_i + INLINE, start_c : start_c + CROSS
    ].astype(jnp.float32)


def forward_conv(grid_x, pad_x, kernel, depth_dev):
    conv = jnp.zeros(grid_x.shape, jnp.float32)
    for offset in range(27):
        conv = conv + kernel[offset] * window(
            pad_x, depth_dev, offset // 9, offset // 3 % 3, offset % 3
        )
    return (grid_x.astype(jnp.float32) + conv).astype(jnp.bfloat16)


def backward_conv(grid_d, pad_d, pad_x, kernel, depth_dev):
    grid_float = grid_d.astype(jnp.float32)
    back = grid_float
    partial_value = []
    for offset in range(27):
        dz, di, dc = (offset // 9, offset // 3 % 3, offset % 3)
        back = back + kernel[offset] * window(pad_d, depth_dev, 2 - dz, 2 - di, 2 - dc)
        partial_value.append(
            jnp.sum(grid_float * window(pad_x, depth_dev, dz, di, dc), axis=(0, 1, 2))
        )
    return (back.astype(jnp.bfloat16), jnp.stack(partial_value))


def shards(tokens, place, kernel, proj_weight, d_projected):
    count = lax.axis_size("seq")
    order = place[0]
    inverse = jnp.argsort(order)
    rows_x = tokens[0]
    d_rows = d_projected[0]
    depth_dev = rows_x.shape[0] // (INLINE * CROSS)
    d_y = lax.dot_general(
        d_rows,
        lax.all_gather(proj_weight, "seq", axis=0, tiled=True),
        (((1,), (1,)), ((), ())),
        preferred_element_type=jnp.float32,
    )
    d_y = d_y.astype(jnp.bfloat16)
    grid_x = to_bricks(rows_x, inverse, count)
    pad_x = with_faces(grid_x)
    grid_y = forward_conv(grid_x, pad_x, kernel, depth_dev)
    rows_y = to_scan(grid_y, order, count)
    grid_d = to_bricks(d_y, inverse, count)
    pad_d = with_faces(grid_d)
    back, partial_value = backward_conv(grid_d, pad_d, pad_x, kernel, depth_dev)
    d_tokens = to_scan(back, order, count)
    projected = jnp.dot(
        rows_y,
        lax.all_gather(proj_weight, "seq", axis=0, tiled=True),
        preferred_element_type=jnp.float32,
    )
    projected = projected.astype(jnp.bfloat16)
    d_kernel = lax.psum(partial_value, ("dp", "seq"))
    return (projected[None], d_tokens[None], d_kernel)


def solution(mesh):
    placed = (P("dp", "seq", None), P("seq", None), P(), P("seq", None), P("dp", "seq", None))
    return jax.shard_map(
        shards,
        mesh=mesh,
        in_specs=placed,
        out_specs=(P("dp", "seq", None), P("dp", "seq", None), P()),
        check_vma=False,
    )
```

profile of v0, /device:TPU:1, one launch (start us, length us, event | category | flops | bytes accessed | tf_op | source)
XLA Modules:
  0.0 491.7 jit_solution(6049392206160936502)
XLA Ops:
  7.2 0.7 all-gather.3.cloned.1.call-update
  7.9 1.8 reshape_squeeze.3
  9.7 11.6 %all-to-all-start = ((bf16[64,2,1280]{2,1,0:T(2,128)(2,1)}), bf16[64,2,1280]{2,1,0:T(2,128)(2,1)S(1)}, u32[]{:S(2)}, u32[]{:S(2)}) async-start(bf16[64,2,1280]{2,1,0:T(2,128)(2,1)} %reshape_squeeze.3), calls=%async_computation | async-start | bytes 655360 | tf_op jit(solution)/shard_map/all_to_all | solution.py:40
  21.4 3.2 sort.17
  24.6 1.9 slice_reduce_fusion.25
  26.5 0.7 compare_select_fusion
  27.1 83.8 %all-gather.3.cloned.1.call-done = bf16[64,20,3840]{2,1,0:T(8,128)(2,1)} async-done(((bf16[1,20,3840]{2,1,0:T(8,128)(2,1)}), bf16[64,20,3840]{2,1,0:T(8,128)(2,1)}) %all-gather.3.cloned.1.call-update) | async-done | bytes 9830416 | tf_op jit(solution)/shard_map/all_gather | solution.py:114
  110.9 13.7 %reshape.119 = bf16[1280,3840]{1,0:T(8,128)(2,1)} reshape(bf16[64,20,3840]{2,1,0:T(8,128)(2,1)} %all-gather.3.cloned.1.call-done) | data formatting | bytes 19660800
  124.6 7.1 %convolution_convert_fusion.1 = bf16[128,1280]{1,0:T(8,128)(2,1)S(1)} fusion(bf16[1280,3840]{1,0:T(8,128)(2,1)} %reshape.119, bf16[1,128,3840]{2,1,0:T(8,128)(2,1)S(1)} %copy-done), kind=kOutput, calls=%fused_computation.41 | convolution fusion | flops 1258455040 | bytes 11141120 | tf_op jit(solution)/shard_map/dot_general | solution.py:97
  131.7 0.9 reshape.77
  132.6 5.7 %all-to-all-start.2 = ((bf16[64,2,1280]{2,1,0:T(2,128)(2,1)}), bf16[64,2,1280]{2,1,0:T(2,128)(2,1)S(1)}, u32[]{:S(2)}, u32[]{:S(2)}) async-start(bf16[64,2,1280]{2,1,0:T(2,128)(2,1)} %reshape.77), calls=%async_computation.2 | async-start | bytes 655360 | tf_op jit(solution)/shard_map/all_to_all | solution.py:40
  138.3 0.6 pad_clamp_fusion
  138.8 0.9 slice_reduce_fusion.26
  139.7 0.5 compare_and_fusion
  140.3 0.9 gather_fusion
  141.2 11.2 %all-to-all-done.2 = bf16[64,2,1280]{2,1,0:T(2,128)(2,1)S(1)} async-done(((bf16[64,2,1280]{2,1,0:T(2,128)(2,1)}), bf16[64,2,1280]{2,1,0:T(2,128)(2,1)S(1)}, u32[]{:S(2)}, u32[]{:S(2)}) %all-to-all-start.2) | async-done | bytes 327712 | tf_op jit(solution)/shard_map/all_to_all | solution.py:40
  152.6 0.9 gather_fusion.2
  153.6 0.8 multiply_reduce_fusion
  154.4 2.1 collective-permute-start.1
  156.5 3.5 collective-permute-start
  160.0 0.7 slice_bitcast_fusion.1
  160.7 1.9 collective-permute-start.2
  162.7 3.1 collective-permute-start.3
  165.8 0.6 select_maximum_fusion.2
  166.5 2.5 fusion.83
  169.0 1.7 gather_fusion.1
  170.7 1.5 select_maximum_fusion
  172.2 3.4 add_convert_fusion
  175.7 1.9 gather_fusion.3
  177.5 1.9 broadcast_select_fusion
  179.5 1.8 reshape.75
  181.3 9.7 %all-to-all-start.1 = ((bf16[64,2,1280]{2,1,0:T(2,128)(2,1)}), bf16[64,2,1280]{2,1,0:T(2,128)(2,1)}, u32[]{:S(2)}, u32[]{:S(2)}) async-start(bf16[64,2,1280]{2,1,0:T(2,128)(2,1)} %reshape.75), calls=%async_computation.1 | async-start | bytes 655360 | tf_op jit(solution)/shard_map/all_to_all | solution.py:51
  190.9 0.6 stack.97
  191.5 0.8 reshape.81
  192.4 2.4 fusion.82
  194.8 10.2 %all-to-all-done.1 = bf16[64,2,1280]{2,1,0:T(2,128)(2,1)} async-done(((bf16[64,2,1280]{2,1,0:T(2,128)(2,1)}), bf16[64,2,1280]{2,1,0:T(2,128)(2,1)}, u32[]{:S(2)}, u32[]{:S(2)}) %all-to-all-start.1) | async-done | bytes 327712 | tf_op jit(solution)/shard_map/all_to_all | solution.py:51
  205.0 5.2 %all-to-all-start.3 = ((bf16[64,2,1280]{2,1,0:T(2,128)(2,1)}), bf16[64,2,1280]{2,1,0:T(2,128)(2,1)}, u32[]{:S(2)}, u32[]{:S(2)}) async-start(bf16[64,2,1280]{2,1,0:T(2,128)(2,1)} %reshape.81), calls=%async_computation.3 | async-start | bytes 655360 | tf_op jit(solution)/shard_map/all_to_all | solution.py:51
  210.3 1.5 fusion.78
  211.9 0.7 stack.110
  212.7 0.7 stack.109
  213.4 0.7 stack.108
  214.1 0.7 stack.107
  215.0 3.4 stack.111
  218.4 1.1 reshape.76
  219.5 6.2 %fusion = bf16[1,128,3840]{2,1,0:T(8,128)(2,1)} fusion(bf16[128,1280]{1,0:T(8,128)(2,1)S(1)} %reshape.76, bf16[1280,3840]{1,0:T(8,128)(2,1)} %reshape.119), kind=kOutput, calls=%fused_computation.37 | convolution fusion | flops 1258782720 | bytes 11141120 | tf_op jit(solution)/shard_map/dot_general | solution.py:112
  225.7 1.8 broadcast_in_dim_reshape.3
  227.5 255.8 %all-reduce.4.cloned.1.call-done = f32[27,1280]{1,0:T(8,128)} async-done(((f32[27,1280]{1,0:T(8,128)}), f32[27,1280]{1,0:T(8,128)}) %all-reduce.4.cloned.1.call-update) | async-done | bytes 138256 | tf_op jit(solution)/shard_map/psum | solution.py:118
  483.3 1.6 copy.9
  (78 shorter events, 0.6 us)
Async XLA Ops:
  7.2 117.5 %copy-start = (bf16[1,128,3840]{2,1,0:T(8,128)(2,1)S(1)}, bf16[1,128,3840]{2,1,0:T(8,128)(2,1)}, u32[]{:S(2)}) copy-start(bf16[1,128,3840]{2,1,0:T(8,128)(2,1)} %param.11) | copy-start | bytes 2949124
  7.2 103.8 %all-gather.3.cloned.1.call-start = ((), (), s32[]{:S(2)}) async-start(), calls=%async_computation.5 | async-start | bytes 11980800 | tf_op jit(solution)/shard_map/all_gather | solution.py:114
  9.7 122.8 %all-to-all-start = ((bf16[64,2,1280]{2,1,0:T(2,128)(2,1)}), bf16[64,2,1280]{2,1,0:T(2,128)(2,1)S(1)}, u32[]{:S(2)}, u32[]{:S(2)}) async-start(bf16[64,2,1280]{2,1,0:T(2,128)(2,1)} %reshape_squeeze.3), calls=%async_computation | async-start | bytes 655360 | tf_op jit(solution)/shard_map/all_to_all | solution.py:40
  124.6 14.2 %copy-start.4 = (f32[27,1280]{1,0:T(8,128)S(1)}, f32[27,1280]{1,0:T(8,128)}, u32[]{:S(2)}) copy-start(f32[27,1280]{1,0:T(8,128)} %param.9) | copy-start | bytes 414724
  124.6 15.1 %copy-start.19 = (s32[1,128]{1,0:T(1,128)S(1)}, s32[1,128]{1,0:T(1,128)}, u32[]{:S(2)}) copy-start(s32[1,128]{1,0:T(1,128)} %param.8) | copy-start | bytes 1540
  132.6 19.9 %all-to-all-start.2 = ((bf16[64,2,1280]{2,1,0:T(2,128)(2,1)}), bf16[64,2,1280]{2,1,0:T(2,128)(2,1)S(1)}, u32[]{:S(2)}, u32[]{:S(2)}) async-start(bf16[64,2,1280]{2,1,0:T(2,128)(2,1)} %reshape.77), calls=%async_computation.2 | async-start | bytes 655360 | tf_op jit(solution)/shard_map/all_to_all | solution.py:40
  153.5 12.9 %copy-start.5 = (f32[1280]{0:T(1024)S(1)}, f32[1280]{0:T(1024)}, u32[]{:S(2)}) copy-start(f32[1280]{0:T(1024)} %get-tuple-element.52) | copy-start | bytes 15364
  153.5 12.9 %copy-start.6 = (f32[1280]{0:T(1024)S(1)}, f32[1280]{0:T(1024)}, u32[]{:S(2)}) copy-start(f32[1280]{0:T(1024)} %get-tuple-element.53) | copy-start | bytes 15364
  153.5 12.9 %copy-start.7 = (f32[1280]{0:T(1024)S(1)}, f32[1280]{0:T(1024)}, u32[]{:S(2)}) copy-start(f32[1280]{0:T(1024)} %get-tuple-element.54) | copy-start | bytes 15364
  153.5 12.9 %copy-start.8 = (f32[1280]{0:T(1024)S(1)}, f32[1280]{0:T(1024)}, u32[]{:S(2)}) copy-start(f32[1280]{0:T(1024)} %get-tuple-element.55) | copy-start | bytes 15364
  153.5 12.9 %copy-start.9 = (f32[1280]{0:T(1024)S(1)}, f32[1280]{0:T(1024)}, u32[]{:S(2)}) copy-start(f32[1280]{0:T(1024)} %get-tuple-element.56) | copy-start | bytes 15364
  153.5 12.9 %copy-start.10 = (f32[1280]{0:T(1024)S(1)}, f32[1280]{0:T(1024)}, u32[]{:S(2)}) copy-start(f32[1280]{0:T(1024)} %get-tuple-element.57) | copy-start | bytes 15364
  153.5 12.9 %copy-start.11 = (f32[1280]{0:T(1024)S(1)}, f32[1280]{0:T(1024)}, u32[]{:S(2)}) copy-start(f32[1280]{0:T(1024)} %get-tuple-element.58) | copy-start | bytes 15364
  153.5 12.9 %copy-start.12 = (f32[1280]{0:T(1024)S(1)}, f32[1280]{0:T(1024)}, u32[]{:S(2)}) copy-start(f32[1280]{0:T(1024)} %get-tuple-element.59) | copy-start | bytes 15364
  153.5 12.9 %copy-start.13 = (f32[1280]{0:T(1024)S(1)}, f32[1280]{0:T(1024)}, u32[]{:S(2)}) copy-start(f32[1280]{0:T(1024)} %get-tuple-element.60) | copy-start | bytes 15364
  153.6 12.9 %copy-start.14 = (f32[1280]{0:T(1024)S(1)}, f32[1280]{0:T(1024)}, u32[]{:S(2)}) copy-start(f32[1280]{0:T(1024)} %get-tuple-element.61) | copy-start | bytes 15364
  153.6 12.9 %copy-start.15 = (f32[1280]{0:T(1024)S(1)}, f32[1280]{0:T(1024)}, u32[]{:S(2)}) copy-start(f32[1280]{0:T(1024)} %get-tuple-element.62) | copy-start | bytes 15364
  153.6 12.9 %copy-start.16 = (f32[1280]{0:T(1024)S(1)}, f32[1280]{0:T(1024)}, u32[]{:S(2)}) copy-start(f32[1280]{0:T(1024)} %get-tuple-element.63) | copy-start | bytes 15364
  153.6 12.9 %copy-start.17 = (f32[1280]{0:T(1024)S(1)}, f32[1280]{0:T(1024)}, u32[]{:S(2)}) copy-start(f32[1280]{0:T(1024)} %get-tuple-element.64) | copy-start | bytes 15364
  154.4 14.5 %copy-start.1 = (bf16[128,1280]{1,0:T(8,128)(2,1)}, bf16[128,1280]{1,0:T(8,128)(2,1)S(1)}, u32[]{:S(2)}) copy-start(bf16[128,1280]{1,0:T(8,128)(2,1)S(1)} %get-tuple-element.67) | copy-start | bytes 983044
  154.4 11.3 %collective-permute-start.1 = (bf16[1,8,8,1280]{3,2,1,0:T(8,128)(2,1)S(1)}, bf16[1,8,8,1280]{3,2,1,0:T(8,128)(2,1)S(1)}, u32[]{:S(2)}, u32[]{:S(2)}) collective-permute-start(bf16[1,8,8,1280]{3,2,1,0:T(8,128)(2,1)S(1)} %get-tuple-element.70), channel_id=1, source_target_pairs={{1,0},{2,1},{3,2},{4,3},{5,4},{6,5},{7,6},{8,7},{9,8},{10,9},{11,1... | collective-permute-start | bytes 491528 | tf_op jit(solution)/shard_map/ppermute | solution.py:18
  156.5 9.2 %collective-permute-start = (bf16[1,8,8,1280]{3,2,1,0:T(8,128)(2,1)S(1)}, bf16[1,8,8,1280]{3,2,1,0:T(8,128)(2,1)S(1)}, u32[]{:S(2)}, u32[]{:S(2)}) collective-permute-start(bf16[1,8,8,1280]{3,2,1,0:T(8,128)(2,1)S(1)} %get-tuple-element.71), channel_id=1, source_target_pairs={{0,1},{1,2},{2,3},{3,4},{4,5},{5,6},{6,7},{7,8},{8,9},{9,10},{10,1... | collective-permute-start | bytes 491528 | tf_op jit(solution)/shard_map/ppermute | solution.py:17
  160.7 10.0 %collective-permute-start.2 = (bf16[1,8,8,1280]{3,2,1,0:T(8,128)(2,1)}, bf16[1,8,8,1280]{3,2,1,0:T(8,128)(2,1)}, u32[]{:S(2)}, u32[]{:S(2)}) collective-permute-start(bf16[1,8,8,1280]{3,2,1,0:T(8,128)(2,1)} %get-tuple-element.68), channel_id=1, source_target_pairs={{0,1},{1,2},{2,3},{3,4},{4,5},{5,6},{6,7},{7,8},{8,9},{9,10},{10,1... | collective-permute-start | bytes 491528 | tf_op jit(solution)/shard_map/ppermute | solution.py:17
  162.7 8.0 %collective-permute-start.3 = (bf16[1,8,8,1280]{3,2,1,0:T(8,128)(2,1)}, bf16[1,8,8,1280]{3,2,1,0:T(8,128)(2,1)}, u32[]{:S(2)}, u32[]{:S(2)}) collective-permute-start(bf16[1,8,8,1280]{3,2,1,0:T(8,128)(2,1)} %get-tuple-element.69), channel_id=1, source_target_pairs={{1,0},{2,1},{3,2},{4,3},{5,4},{6,5},{7,6},{8,7},{9,8},{10,9},{11,1... | collective-permute-start | bytes 491528 | tf_op jit(solution)/shard_map/ppermute | solution.py:18
  165.7 3.2 copy-start.3
  175.6 15.3 %copy-start.18 = (f32[1280]{0:T(1024)S(1)}, f32[1280]{0:T(1024)}, u32[]{:S(2)}) copy-start(f32[1280]{0:T(1024)} %get-tuple-element.65) | copy-start | bytes 15364
  181.3 23.8 %all-to-all-start.1 = ((bf16[64,2,1280]{2,1,0:T(2,128)(2,1)}), bf16[64,2,1280]{2,1,0:T(2,128)(2,1)}, u32[]{:S(2)}, u32[]{:S(2)}) async-start(bf16[64,2,1280]{2,1,0:T(2,128)(2,1)} %reshape.75), calls=%async_computation.1 | async-start | bytes 655360 | tf_op jit(solution)/shard_map/all_to_all | solution.py:51
  192.4 18.0 %copy-start.2 = (bf16[128,1280]{1,0:T(8,128)(2,1)S(1)}, bf16[128,1280]{1,0:T(8,128)(2,1)}, u32[]{:S(2)}) copy-start(bf16[128,1280]{1,0:T(8,128)(2,1)} %copy-done.1) | copy-start | bytes 983044
  205.0 20.6 %all-to-all-start.3 = ((bf16[64,2,1280]{2,1,0:T(2,128)(2,1)}), bf16[64,2,1280]{2,1,0:T(2,128)(2,1)}, u32[]{:S(2)}, u32[]{:S(2)}) async-start(bf16[64,2,1280]{2,1,0:T(2,128)(2,1)} %reshape.81), calls=%async_computation.3 | async-start | bytes 655360 | tf_op jit(solution)/shard_map/all_to_all | solution.py:51
  210.3 273.0 %all-reduce.4.cloned.1.call-start = ((), (), s32[]{:S(2)}) async-start(), calls=%async_computation.4 | async-start | bytes 327680 | tf_op jit(solution)/shard_map/psum | solution.py:118
Sparse Core Ops, SparseCore 0:
  11.3 99.6 all-gather.2
  218.5 264.7 all-reduce.3
where the time goes:
time: 493 us; the launch traced here: 492 us
  waiting for transfers between devices  362 us (73%)
  starting transfers between devices  42.8 us (9%)
  local copies, waits for them, and re-layouts  39.6 us (8%)
  other arithmetic  19.6 us (4%)
  between operations  14.6 us (3%)
  matrix products  13.3 us (3%)
    psum x1, waiting for transfers between devices, shards(): d_kernel = lax.psum(partial_value, ('dp', 'seq'))  256 us
    all_gather x1, waiting for transfers between devices, shards(): lax.all_gather(proj_weight, 'seq', axis=0, tiled=True)  83.8 us
    all_to_all x2, starting transfers between devices, to_bricks(): lax.all_to_all(rows.reshape(count, tokens_dev // count, width), 'seq', sp...  17.3 us
    unnamed x42, local copies, waits for them, and re-layouts  15.4 us
    all_to_all x2, starting transfers between devices, to_scan(): lax.all_to_all(scan_pieces(cells, order, count), 'seq', split_axis=0, con...  14.9 us
    all_to_all x2, waiting for transfers between devices, to_bricks(): lax.all_to_all(rows.reshape(count, tokens_dev // count, width), 'seq', sp...  11.2 us
    all_to_all x2, waiting for transfers between devices, to_scan(): lax.all_to_all(scan_pieces(cells, order, count), 'seq', split_axis=0, con...  10.3 us
  transfers between devices with their start and end apart: 10, of which 4 were waited for; matrix products, arithmetic and copies ran while one was open for 12% of the time, Pallas kernels for 0%

commit v1 on v0

--- a/solution.py
+++ b/solution.py
@@ -115,7 +115,7 @@
         preferred_element_type=jnp.float32,
     )
     projected = projected.astype(jnp.bfloat16)
-    d_kernel = lax.psum(partial_value, ("dp", "seq"))
+    d_kernel = lax.psum(lax.psum(partial_value, "seq"), "dp")
     return (projected[None], d_tokens[None], d_kernel)
 
 

time: 493 us -> 473 us (0.959)
  waiting for transfers between devices: 362 us -> 345 us
    psum x1 -> x2, waiting for transfers between devices: 256 us -> 242 us  [shards(): d_kernel = lax.psum(lax.psum(partial_value, 'seq'), 'dp')]
    unnamed x42 -> x44, local copies, waits for them, and re-layouts: 15.4 us -> 15.4 us
  transfers between devices with their start and end apart: 10 -> 11, of which waited for: 4 -> 5; matrix products, arithmetic and copies ran while one was open for 12% -> 11% of each run, Pallas kernels for 0% -> 0%
where the time goes in v1:
time: 473 us; the launch traced here: 468 us
  waiting for transfers between devices  345 us (73%)
  starting transfers between devices  42.7 us (9%)
  local copies, waits for them, and re-layouts  35 us (7%)
  other arithmetic  17.6 us (4%)
  between operations  14.4 us (3%)
  matrix products  13.3 us (3%)
    psum x2, waiting for transfers between devices, shards(): d_kernel = lax.psum(lax.psum(partial_value, 'seq'), 'dp')  242 us
    all_gather x1, waiting for transfers between devices, shards(): lax.all_gather(proj_weight, 'seq', axis=0, tiled=True)  83.9 us
    all_to_all x2, starting transfers between devices, to_bricks(): lax.all_to_all(rows.reshape(count, tokens_dev // count, width), 'seq', sp...  17.3 us
    unnamed x44, local copies, waits for them, and re-layouts  15.4 us
    all_to_all x2, starting transfers between devices, to_scan(): lax.all_to_all(scan_pieces(cells, order, count), 'seq', split_axis=0, con...  14.7 us
    all_to_all x2, waiting for transfers between devices, to_bricks(): lax.all_to_all(rows.reshape(count, tokens_dev // count, width), 'seq', sp...  11.1 us
  transfers between devices with their start and end apart: 11, of which 5 were waited for; matrix products, arithmetic and copies ran while one was open for 11% of the time, Pallas kernels for 0%

profile of v1, /device:TPU:1, one launch (start us, length us, event | category | flops | bytes accessed | tf_op | source)
XLA Modules:
  0.0 467.6 jit_solution(5241495999294572101)
XLA Ops:
  7.2 0.7 all-gather.3.cloned.1.call-update
  7.9 1.8 reshape_squeeze.3
  9.7 11.6 %all-to-all-start = ((bf16[64,2,1280]{2,1,0:T(2,128)(2,1)}), bf16[64,2,1280]{2,1,0:T(2,128)(2,1)S(1)}, u32[]{:S(2)}, u32[]{:S(2)}) async-start(bf16[64,2,1280]{2,1,0:T(2,128)(2,1)} %reshape_squeeze.3), calls=%async_computation | async-start | bytes 655360 | tf_op jit(solution)/shard_map/all_to_all | solution.py:40
  21.4 3.2 sort.17
  24.6 1.8 slice_reduce_fusion.25
  26.4 0.7 compare_select_fusion
  27.0 83.9 %all-gather.3.cloned.1.call-done = bf16[64,20,3840]{2,1,0:T(8,128)(2,1)} async-done(((bf16[1,20,3840]{2,1,0:T(8,128)(2,1)}), bf16[64,20,3840]{2,1,0:T(8,128)(2,1)}) %all-gather.3.cloned.1.call-update) | async-done | bytes 9830416 | tf_op jit(solution)/shard_map/all_gather | solution.py:114
  110.9 13.7 %reshape.119 = bf16[1280,3840]{1,0:T(8,128)(2,1)} reshape(bf16[64,20,3840]{2,1,0:T(8,128)(2,1)} %all-gather.3.cloned.1.call-done) | data formatting | bytes 19660800
  124.6 7.1 %convolution_convert_fusion.1 = bf16[128,1280]{1,0:T(8,128)(2,1)S(1)} fusion(bf16[1280,3840]{1,0:T(8,128)(2,1)} %reshape.119, bf16[1,128,3840]{2,1,0:T(8,128)(2,1)S(1)} %copy-done), kind=kOutput, calls=%fused_computation.41 | convolution fusion | flops 1258455040 | bytes 11141120 | tf_op jit(solution)/shard_map/dot_general | solution.py:97
  131.7 0.9 reshape.77
  132.6 5.7 %all-to-all-start.2 = ((bf16[64,2,1280]{2,1,0:T(2,128)(2,1)}), bf16[64,2,1280]{2,1,0:T(2,128)(2,1)S(1)}, u32[]{:S(2)}, u32[]{:S(2)}) async-start(bf16[64,2,1280]{2,1,0:T(2,128)(2,1)} %reshape.77), calls=%async_computation.2 | async-start | bytes 655360 | tf_op jit(solution)/shard_map/all_to_all | solution.py:40
  138.3 0.6 pad_clamp_fusion
  138.9 0.9 slice_reduce_fusion.26
  139.7 0.6 compare_and_fusion
  140.3 0.1 reshape.72
  140.4 0.9 gather_fusion
  141.3 11.1 %all-to-all-done.2 = bf16[64,2,1280]{2,1,0:T(2,128)(2,1)S(1)} async-done(((bf16[64,2,1280]{2,1,0:T(2,128)(2,1)}), bf16[64,2,1280]{2,1,0:T(2,128)(2,1)S(1)}, u32[]{:S(2)}, u32[]{:S(2)}) %all-to-all-start.2) | async-done | bytes 327712 | tf_op jit(solution)/shard_map/all_to_all | solution.py:40
  152.4 0.1 reshape.78
  152.6 0.9 gather_fusion.2
  153.6 0.2 multiply_reduce_fusion
  153.9 2.1 collective-permute-start.1
  156.0 3.5 collective-permute-start
  159.5 0.7 slice_bitcast_fusion.1
  160.2 0.6 stack.97
  160.8 1.9 collective-permute-start.2
  162.7 3.1 collective-permute-start.3
  165.8 0.6 select_maximum_fusion.2
  166.5 2.5 fusion.83
  169.0 1.7 gather_fusion.1
  170.8 1.5 select_maximum_fusion
  172.3 3.4 add_convert_fusion
  175.7 1.7 gather_fusion.3
  177.4 1.9 broadcast_select_fusion
  179.4 0.8 reshape.75
  180.2 9.7 %all-to-all-start.1 = ((bf16[64,2,1280]{2,1,0:T(2,128)(2,1)}), bf16[64,2,1280]{2,1,0:T(2,128)(2,1)}, u32[]{:S(2)}, u32[]{:S(2)}) async-start(bf16[64,2,1280]{2,1,0:T(2,128)(2,1)} %reshape.75), calls=%async_computation.1 | async-start | bytes 655360 | tf_op jit(solution)/shard_map/all_to_all | solution.py:51
  189.9 1.8 fusion.82
  191.8 0.6 fusion.78
  192.8 2.7 stack.111
  195.5 1.8 reshape.81
  197.3 6.7 %all-to-all-done.1 = bf16[64,2,1280]{2,1,0:T(2,128)(2,1)} async-done(((bf16[64,2,1280]{2,1,0:T(2,128)(2,1)}), bf16[64,2,1280]{2,1,0:T(2,128)(2,1)}, u32[]{:S(2)}, u32[]{:S(2)}) %all-to-all-start.1) | async-done | bytes 327712 | tf_op jit(solution)/shard_map/all_to_all | solution.py:51
  204.0 5.1 %all-to-all-start.3 = ((bf16[64,2,1280]{2,1,0:T(2,128)(2,1)}), bf16[64,2,1280]{2,1,0:T(2,128)(2,1)S(1)}, u32[]{:S(2)}, u32[]{:S(2)}) async-start(bf16[64,2,1280]{2,1,0:T(2,128)(2,1)} %reshape.81), calls=%async_computation.3 | async-start | bytes 655360 | tf_op jit(solution)/shard_map/all_to_all | solution.py:51
  209.1 0.0 all-reduce.7.cloned.1.call-start
  209.1 175.1 %all-reduce.5.cloned.1.call-done = f32[27,1280]{1,0:T(8,128)} async-done(((f32[27,1280]{1,0:T(8,128)}), f32[27,1280]{1,0:T(8,128)}) %all-reduce.5.cloned.1.call-update) | async-done | bytes 138256 | tf_op jit(solution)/shard_map/psum | solution.py:118
  384.3 1.1 reshape.76
  385.4 6.2 %fusion = bf16[1,128,3840]{2,1,0:T(8,128)(2,1)} fusion(bf16[128,1280]{1,0:T(8,128)(2,1)S(1)} %reshape.76, bf16[1280,3840]{1,0:T(8,128)(2,1)} %reshape.119), kind=kOutput, calls=%fused_computation.37 | convolution fusion | flops 1258782720 | bytes 11141120 | tf_op jit(solution)/shard_map/dot_general | solution.py:112
  391.6 0.8 broadcast_in_dim_reshape.3
  392.4 67.0 %all-reduce.7.cloned.1.call-done = f32[27,1280]{1,0:T(8,128)} async-done(((f32[27,1280]{1,0:T(8,128)}), f32[27,1280]{1,0:T(8,128)}) %all-reduce.7.cloned.1.call-update) | async-done | bytes 138256 | tf_op jit(solution)/shard_map/psum | solution.py:118
  459.5 1.6 copy.10
  (83 shorter events, 0.4 us)
Async XLA Ops:
  7.2 117.5 %copy-start = (bf16[1,128,3840]{2,1,0:T(8,128)(2,1)S(1)}, bf16[1,128,3840]{2,1,0:T(8,128)(2,1)}, u32[]{:S(2)}) copy-start(bf16[1,128,3840]{2,1,0:T(8,128)(2,1)} %param.11) | copy-start | bytes 2949124
  7.2 103.8 %all-gather.3.cloned.1.call-start = ((), (), s32[]{:S(2)}) async-start(), calls=%async_computation.6 | async-start | bytes 11980800 | tf_op jit(solution)/shard_map/all_gather | solution.py:114
  9.7 122.8 %all-to-all-start = ((bf16[64,2,1280]{2,1,0:T(2,128)(2,1)}), bf16[64,2,1280]{2,1,0:T(2,128)(2,1)S(1)}, u32[]{:S(2)}, u32[]{:S(2)}) async-start(bf16[64,2,1280]{2,1,0:T(2,128)(2,1)} %reshape_squeeze.3), calls=%async_computation | async-start | bytes 655360 | tf_op jit(solution)/shard_map/all_to_all | solution.py:40
  124.6 14.2 %copy-start.5 = (f32[27,1280]{1,0:T(8,128)S(1)}, f32[27,1280]{1,0:T(8,128)}, u32[]{:S(2)}) copy-start(f32[27,1280]{1,0:T(8,128)} %param.9) | copy-start | bytes 414724
  124.6 15.1 %copy-start.20 = (s32[1,128]{1,0:T(1,128)S(1)}, s32[1,128]{1,0:T(1,128)}, u32[]{:S(2)}) copy-start(s32[1,128]{1,0:T(1,128)} %param.8) | copy-start | bytes 1540
  132.6 19.9 %all-to-all-start.2 = ((bf16[64,2,1280]{2,1,0:T(2,128)(2,1)}), bf16[64,2,1280]{2,1,0:T(2,128)(2,1)S(1)}, u32[]{:S(2)}, u32[]{:S(2)}) async-start(bf16[64,2,1280]{2,1,0:T(2,128)(2,1)} %reshape.77), calls=%async_computation.2 | async-start | bytes 655360 | tf_op jit(solution)/shard_map/all_to_all | solution.py:40
  153.5 12.9 %copy-start.6 = (f32[1280]{0:T(1024)S(1)}, f32[1280]{0:T(1024)}, u32[]{:S(2)}) copy-start(f32[1280]{0:T(1024)} %get-tuple-element.52) | copy-start | bytes 15364
  153.5 12.9 %copy-start.7 = (f32[1280]{0:T(1024)S(1)}, f32[1280]{0:T(1024)}, u32[]{:S(2)}) copy-start(f32[1280]{0:T(1024)} %get-tuple-element.53) | copy-start | bytes 15364
  153.5 12.9 %copy-start.8 = (f32[1280]{0:T(1024)S(1)}, f32[1280]{0:T(1024)}, u32[]{:S(2)}) copy-start(f32[1280]{0:T(1024)} %get-tuple-element.54) | copy-start | bytes 15364
  153.5 12.9 %copy-start.9 = (f32[1280]{0:T(1024)S(1)}, f32[1280]{0:T(1024)}, u32[]{:S(2)}) copy-start(f32[1280]{0:T(1024)} %get-tuple-element.55) | copy-start | bytes 15364
  153.5 12.9 %copy-start.10 = (f32[1280]{0:T(1024)S(1)}, f32[1280]{0:T(1024)}, u32[]{:S(2)}) copy-start(f32[1280]{0:T(1024)} %get-tuple-element.56) | copy-start | bytes 15364
  153.5 12.9 %copy-start.11 = (f32[1280]{0:T(1024)S(1)}, f32[1280]{0:T(1024)}, u32[]{:S(2)}) copy-start(f32[1280]{0:T(1024)} %get-tuple-element.57) | copy-start | bytes 15364
  153.5 12.9 %copy-start.12 = (f32[1280]{0:T(1024)S(1)}, f32[1280]{0:T(1024)}, u32[]{:S(2)}) copy-start(f32[1280]{0:T(1024)} %get-tuple-element.58) | copy-start | bytes 15364
  153.5 12.9 %copy-start.13 = (f32[1280]{0:T(1024)S(1)}, f32[1280]{0:T(1024)}, u32[]{:S(2)}) copy-start(f32[1280]{0:T(1024)} %get-tuple-element.59) | copy-start | bytes 15364
  153.5 12.9 %copy-start.14 = (f32[1280]{0:T(1024)S(1)}, f32[1280]{0:T(1024)}, u32[]{:S(2)}) copy-start(f32[1280]{0:T(1024)} %get-tuple-element.60) | copy-start | bytes 15364
  153.6 12.9 %copy-start.15 = (f32[1280]{0:T(1024)S(1)}, f32[1280]{0:T(1024)}, u32[]{:S(2)}) copy-start(f32[1280]{0:T(1024)} %get-tuple-element.61) | copy-start | bytes 15364
  153.6 12.9 %copy-start.16 = (f32[1280]{0:T(1024)S(1)}, f32[1280]{0:T(1024)}, u32[]{:S(2)}) copy-start(f32[1280]{0:T(1024)} %get-tuple-element.62) | copy-start | bytes 15364
  153.6 12.9 %copy-start.17 = (f32[1280]{0:T(1024)S(1)}, f32[1280]{0:T(1024)}, u32[]{:S(2)}) copy-start(f32[1280]{0:T(1024)} %get-tuple-element.63) | copy-start | bytes 15364
  153.6 12.9 %copy-start.18 = (f32[1280]{0:T(1024)S(1)}, f32[1280]{0:T(1024)}, u32[]{:S(2)}) copy-start(f32[1280]{0:T(1024)} %get-tuple-element.64) | copy-start | bytes 15364
  153.8 15.2 %copy-start.1 = (bf16[128,1280]{1,0:T(8,128)(2,1)}, bf16[128,1280]{1,0:T(8,128)(2,1)S(1)}, u32[]{:S(2)}) copy-start(bf16[128,1280]{1,0:T(8,128)(2,1)S(1)} %get-tuple-element.67) | copy-start | bytes 983044
  153.9 11.9 %collective-permute-start.1 = (bf16[1,8,8,1280]{3,2,1,0:T(8,128)(2,1)S(1)}, bf16[1,8,8,1280]{3,2,1,0:T(8,128)(2,1)S(1)}, u32[]{:S(2)}, u32[]{:S(2)}) collective-permute-start(bf16[1,8,8,1280]{3,2,1,0:T(8,128)(2,1)S(1)} %get-tuple-element.70), channel_id=1, source_target_pairs={{1,0},{2,1},{3,2},{4,3},{5,4},{6,5},{7,6},{8,7},{9,8},{10,9},{11,1... | collective-permute-start | bytes 491528 | tf_op jit(solution)/shard_map/ppermute | solution.py:18
  156.0 9.8 %collective-permute-start = (bf16[1,8,8,1280]{3,2,1,0:T(8,128)(2,1)S(1)}, bf16[1,8,8,1280]{3,2,1,0:T(8,128)(2,1)S(1)}, u32[]{:S(2)}, u32[]{:S(2)}) collective-permute-start(bf16[1,8,8,1280]{3,2,1,0:T(8,128)(2,1)S(1)} %get-tuple-element.71), channel_id=1, source_target_pairs={{0,1},{1,2},{2,3},{3,4},{4,5},{5,6},{6,7},{7,8},{8,9},{9,10},{10,1... | collective-permute-start | bytes 491528 | tf_op jit(solution)/shard_map/ppermute | solution.py:17
  160.8 10.0 %collective-permute-start.2 = (bf16[1,8,8,1280]{3,2,1,0:T(8,128)(2,1)}, bf16[1,8,8,1280]{3,2,1,0:T(8,128)(2,1)}, u32[]{:S(2)}, u32[]{:S(2)}) collective-permute-start(bf16[1,8,8,1280]{3,2,1,0:T(8,128)(2,1)} %get-tuple-element.68), channel_id=1, source_target_pairs={{0,1},{1,2},{2,3},{3,4},{4,5},{5,6},{6,7},{7,8},{8,9},{9,10},{10,1... | collective-permute-start | bytes 491528 | tf_op jit(solution)/shard_map/ppermute | solution.py:17
  162.7 8.0 %collective-permute-start.3 = (bf16[1,8,8,1280]{3,2,1,0:T(8,128)(2,1)}, bf16[1,8,8,1280]{3,2,1,0:T(8,128)(2,1)}, u32[]{:S(2)}, u32[]{:S(2)}) collective-permute-start(bf16[1,8,8,1280]{3,2,1,0:T(8,128)(2,1)} %get-tuple-element.69), channel_id=1, source_target_pairs={{1,0},{2,1},{3,2},{4,3},{5,4},{6,5},{7,6},{8,7},{9,8},{10,9},{11,1... | collective-permute-start | bytes 491528 | tf_op jit(solution)/shard_map/ppermute | solution.py:18
  165.8 3.2 copy-start.3
  180.2 23.8 %all-to-all-start.1 = ((bf16[64,2,1280]{2,1,0:T(2,128)(2,1)}), bf16[64,2,1280]{2,1,0:T(2,128)(2,1)}, u32[]{:S(2)}, u32[]{:S(2)}) async-start(bf16[64,2,1280]{2,1,0:T(2,128)(2,1)} %reshape.75), calls=%async_computation.1 | async-start | bytes 655360 | tf_op jit(solution)/shard_map/all_to_all | solution.py:51
  189.9 1.9 copy-start.2
  189.9 194.4 %all-reduce.5.cloned.1.call-start = ((), (), s32[]{:S(2)}) async-start(), calls=%async_computation.4 | async-start | bytes 327680 | tf_op jit(solution)/shard_map/psum | solution.py:118
  189.9 1.9 copy-start.4
  191.8 1.0 copy-start.19
  204.0 187.6 %all-to-all-start.3 = ((bf16[64,2,1280]{2,1,0:T(2,128)(2,1)}), bf16[64,2,1280]{2,1,0:T(2,128)(2,1)S(1)}, u32[]{:S(2)}, u32[]{:S(2)}) async-start(bf16[64,2,1280]{2,1,0:T(2,128)(2,1)} %reshape.81), calls=%async_computation.3 | async-start | bytes 655360 | tf_op jit(solution)/shard_map/all_to_all | solution.py:51
  209.1 250.4 %all-reduce.7.cloned.1.call-start = ((), (), s32[]{:S(2)}) async-start(), calls=%async_computation.5 | async-start | bytes 327680 | tf_op jit(solution)/shard_map/psum | solution.py:118
Sparse Core Ops, SparseCore 0:
  11.3 99.6 all-gather.2
  195.6 188.6 all-reduce.4
  386.6 72.8 all-reduce.6
